TPU v7x, 32 devices: a whole 2x2x4 slice. The times are simulated.
32 devices in a mesh: groups: 2 (over x), dp: 2 (over core), fsdp: 8 (over z, y).
Axes of the slice: x: 2, y: 2, z: 4, core: 2. Of those that a mesh axis runs over, the one named last changes fastest.
Arguments:
- output_gradient: bfloat16 [28672, 2880], P(('groups', 'dp', 'fsdp')), parts along dimension 0, may hold values from -6 to 6
- hidden: bfloat16 [28672, 1536], P(('groups', 'dp', 'fsdp')), parts along dimension 0, may hold values from -6 to 6
- gates: float32 [28672], P(('groups', 'dp', 'fsdp')), parts along dimension 0, may hold values from 0.1 to 1
- counts: int32 [32, 2], P(('groups', 'dp', 'fsdp')), parts along dimension 0, may hold values from 1 to 672, 896 in all within a row
- values: bfloat16 [2, 1536, 2880], P(None, None, 'fsdp'), may hold values from -0.15625 to 0.15625
- scales: bfloat16 [2, 48, 2880], P(None, None, 'fsdp'), may hold values from 0.5 to 2, as said below
- adapter_input_maps: bfloat16 [4, 1536, 64], P('groups'), parts along dimension 0, may hold values from -0.15625 to 0.15625
- adapter_output_maps: bfloat16 [4, 64, 2880], P('groups'), parts along dimension 0, may hold values from -0.75 to 0.75
Outputs:
- grad_hidden: bfloat16 [28672, 1536], P(('groups', 'dp', 'fsdp')), parts along dimension 0
- grad_a: float32 [4, 1536, 64], P('groups', 'fsdp'), parts along dimension 0
- grad_b: float32 [4, 64, 2880], P('groups', None, 'fsdp'), parts along dimension 0
There are 2 independent parts, one for each index of `groups`. A program takes and returns all parts, laid end to end along the dimension named above; an argument that names none is the same for every part. Nothing has to cross between parts.
Inputs may be any that keep to these rules, and one draw needn't show every extreme that they name: `counts`: each row sums to 896; no entry exceeds 672. `scales`: every entry is 0.5, 1 or 2.
All inputs are finite; a program needn't handle non-finite values.
Results may differ from a plain program's by a relative error of at most 0.0051.
Values may be sent and summed in bfloat16 or wider, within the bound.
A program may use at most 128 MiB of HBM per device.

v0:
```python
import jax
import jax.numpy as jnp
from jax import lax
from jax.sharding import PartitionSpec as P

HIDDEN_UNITS = 1536
EXPERTS_ACTIVE = 2
CAP = 672


adapter_scale = 0.25


def expert_slices(row_data, offsets, capacity):
    padding = jnp.zeros((capacity,) + row_data.shape[1:], row_data.dtype)
    padded = jnp.concatenate([row_data, padding], axis=0)
    return jnp.stack(
        [
            lax.dynamic_slice_in_dim(padded, offsets[expert], capacity, 0)
            for expert in range(offsets.shape[0])
        ]
    )


def dequantize(block_values, block_scales):
    experts, hidden_rows, columns = block_values.shape
    blocks = block_scales.shape[1]
    shaped = block_values.reshape(experts, blocks, hidden_rows // blocks, columns)
    return (shaped * block_scales[:, :, None, :]).reshape(experts, hidden_rows, columns)


def per_device(
    output_gradient, hidden, gates, counts, values, scales, adapter_input_maps, adapter_output_maps
):
    count_row = counts[0]
    offsets = jnp.cumsum(count_row) - count_row
    gated_rows = (gates[:, None] * output_gradient.astype(jnp.float32)).astype(jnp.bfloat16)
    live_mask = lax.broadcasted_iota(jnp.int32, (EXPERTS_ACTIVE, CAP), 1) < count_row[:, None]
    slot_gradients = jnp.where(
        live_mask[:, :, None], expert_slices(gated_rows, offsets, CAP), jnp.zeros((), jnp.bfloat16)
    )
    slot_hidden_units = expert_slices(hidden, offsets, CAP)
    halves = lax.axis_size("dp")
    share_rows = HIDDEN_UNITS // halves
    share_blocks = scales.shape[1] // halves
    position = lax.axis_index("dp")
    own_values = lax.dynamic_slice_in_dim(values, position * share_rows, share_rows, 1)
    own_scales = lax.dynamic_slice_in_dim(scales, position * share_blocks, share_blocks, 1)
    full_values, full_scales = (
        lax.all_gather(own_values, "fsdp", axis=2, tiled=True),
        lax.all_gather(own_scales, "fsdp", axis=2, tiled=True),
    )
    half_weights = dequantize(full_values, full_scales)
    passthrough_gradient = jnp.einsum(
        "ecd,end->ecn",
        slot_gradients,
        lax.all_gather(half_weights, "dp", axis=1, tiled=True),
        preferred_element_type=jnp.float32,
    )
    rank_input = jnp.einsum(
        "fik,fkb->fib", slot_hidden_units, adapter_input_maps, preferred_element_type=jnp.float32
    ).astype(jnp.bfloat16)
    rank_gradient = jnp.einsum(
        "xoy,xby->xob", slot_gradients, adapter_output_maps, preferred_element_type=jnp.float32
    ).astype(jnp.bfloat16)
    slot_output_rows = passthrough_gradient + adapter_scale * jnp.einsum(
        "swm,skm->swk", rank_gradient, adapter_input_maps, preferred_element_type=jnp.float32
    )
    input_map_term = adapter_scale * jnp.einsum(
        "ino,inx->iox", slot_hidden_units, rank_gradient, preferred_element_type=jnp.float32
    )
    output_map_term = adapter_scale * jnp.einsum(
        "lzq,lzv->lqv", rank_input, slot_gradients, preferred_element_type=jnp.float32
    )
    rows_here = output_gradient.shape[0]
    assembled = jnp.zeros((rows_here + CAP, HIDDEN_UNITS), jnp.float32)
    for expert in range(EXPERTS_ACTIVE):
        current = lax.dynamic_slice_in_dim(assembled, offsets[expert], CAP, 0)
        assembled = lax.dynamic_update_slice_in_dim(
            assembled, current + slot_output_rows[expert], offsets[expert], 0
        )
    grad_hidden = assembled[:rows_here].astype(jnp.bfloat16)
    share_a, share_b = (
        lax.psum_scatter(input_map_term, "fsdp", scatter_dimension=1, tiled=True),
        lax.psum_scatter(output_map_term, "fsdp", scatter_dimension=2, tiled=True),
    )
    grad_a, grad_b = lax.psum((share_a, share_b), "dp")
    return (grad_hidden, grad_a, grad_b)


def solution(mesh):
    placed = (
        P(("groups", "dp", "fsdp"), None),
        P(("groups", "dp", "fsdp"), None),
        P(("groups", "dp", "fsdp")),
        P(("groups", "dp", "fsdp"), None),
        P(None, None, "fsdp"),
        P(None, None, "fsdp"),
        P("groups", None, None),
        P("groups", None, None),
    )
    return jax.shard_map(
        per_device,
        mesh=mesh,
        in_specs=placed,
        out_specs=(
            P(("groups", "dp", "fsdp"), None),
            P("groups", "fsdp", None),
            P("groups", None, "fsdp"),
        ),
        check_vma=False,
    )
```

profile of v0, /device:TPU:16, one launch (start us, length us, event | category | flops | bytes accessed | tf_op | source)
XLA Modules:
  0.0 433.8 jit_solution(6065248364808707407)
XLA Ops:
  7.2 0.0 all-gather.3.cloned.1.call-start
  7.2 1.6 copy-done
  8.8 1.1 constant_dynamic-slice_fusion.1
  9.9 0.0 all-gather.3.cloned.1.call-update
  9.9 0.0 all-reduce.7.cloned.1.call-start
  9.9 0.8 reduce-window.9
  10.8 0.7 bitcast_subtract_fusion
  11.4 0.6 fusion.15
  15.9 3.5 multiply_convert_fusion
  19.4 7.3 %pad_dynamic-slice_fusion.1 = (bf16[672,2880]{0,1:T(8,128)(2,1)}, bf16[672,2880]{0,1:T(8,128)(2,1)}) fusion(s32[]{:T(128)S(6)} %select_n.21, bf16[896,2880]{0,1:T(8,128)(2,1)S(1)} %multiply_convert_fusion, s32[]{:T(128)S(6)} %select_n.22), kind=kLoop, calls=%fused_computation.1 | loop fusion | bytes 12902408 | tf_op jit(solution)/shard_map/dynamic_slice | solution.py:19
  26.6 6.4 %copy.18 = bf16[672,2880]{1,0:T(8,128)(2,1)} copy(bf16[672,2880]{0,1:T(8,128)(2,1)} %get-tuple-element.5) | data formatting | bytes 7741440 | tf_op jit(solution)/shard_map/dynamic_slice | solution.py:19
  33.0 6.4 %copy.19 = bf16[672,2880]{1,0:T(8,128)(2,1)} copy(bf16[672,2880]{0,1:T(8,128)(2,1)} %get-tuple-element.6) | data formatting | bytes 7741440 | tf_op jit(solution)/shard_map/dynamic_slice | solution.py:19
  39.4 0.1 iota_compare_fusion
  39.5 5.8 %fusion.4 = (bf16[1,672,1536]{2,1,0:T(8,128)(2,1)S(1)}, bf16[1,672,1536]{2,1,0:T(8,128)(2,1)}) fusion(s32[]{:T(128)S(6)} %select_n.21, bf16[896,1536]{1,0:T(8,128)(2,1)} %param.9, s32[]{:T(128)S(6)} %select_n.22), kind=kLoop, calls=%fused_computation.16 | loop fusion | bytes 6881288 | tf_op jit(solution)/shard_map/stack | solution.py:17
  45.3 8.2 %convolution_multiply_fusion = f32[2,64,2880]{2,1,0:T(8,128)} fusion(bf16[2,1536,64]{1,2,0:T(8,128)(2,1)S(1)} %copy-done.3, bf16[1,672,1536]{2,1,0:T(8,128)(2,1)} %get-tuple-element.8, bf16[1,672,1536]{2,1,0:T(8,128)(2,1)S(1)} %get-tuple-element.7, bf16[1,672,2880]{2,1,0:T(8,128)(2,1)} %bitcast.37, bf16[1,672,2880]{2,1,0:T(8,128)(2,1)} %bitcast.34, ...), kind=kOutput, calls=%fused_computation.12 | convolution fusion | flops 769953792 | bytes 13739328 | tf_op jit(solution)/shard_map/lzq,lzv->lqv/dot_general | solution.py:72
  53.5 0.2 reduce-scatter.5.cloned.1.call-start
  53.7 6.1 %convolution_convert_fusion = bf16[2,672,64]{1,2,0:T(8,128)(2,1)S(1)} fusion(bf16[2,64,2880]{2,1,0:T(8,128)(2,1)S(1)} %copy-done.8, bf16[1,672,2880]{2,1,0:T(8,128)(2,1)} %bitcast.38, bf16[1,672,2880]{2,1,0:T(8,128)(2,1)} %bitcast.35, pred[2,672]{1,0:T(4,128)(4,1)S(1)} %iota_compare_fusion), kind=kOutput, calls=%fused_computation.19 | convolution fusion | flops 503279616 | bytes 8652096 | tf_op jit(solution)/shard_map/xoy,xby->xob/dot_general | solution.py:63
  59.8 0.7 copy-done.4
  60.5 1.0 fusion.3
  61.5 0.8 copy.23
  62.3 1.8 reshape.62
  64.1 0.0 all-gather.5.cloned.1.call-start
  64.2 0.2 copy.27
  64.4 45.8 %all_gather.10 = bf16[2,24,2880]{1,0,2:T(2,128)(2,1)S(1)} all-gather(bf16[2,24,360]{1,0,2:T(2,128)(2,1)S(1)} %copy.27), channel_id=1, replica_groups=mesh['groups'=2,'dp'=2,'fsdp'=8] {'fsdp'}, dimensions={2}, use_global_device_ids=true | all-gather | bytes 311040 | tf_op jit(solution)/shard_map/all_gather | solution.py:51
  110.2 1.7 copy.21
  111.9 4.1 mul.47
  116.0 11.9 %copy.22 = bf16[2,768,2880]{1,2,0:T(8,128)(2,1)} copy(bf16[2,768,2880]{2,1,0:T(8,128)(2,1)} %bitcast.32) | data formatting | bytes 17694720 | tf_op jit(solution)/shard_map/mul | solution.py:29
  127.9 41.4 %all-gather.3.cloned.1.call-done = bf16[2,768,2880]{1,2,0:T(8,128)(2,1)} async-done(((bf16[2,768,360]{1,2,0:T(8,128)(2,1)}), bf16[2,768,2880]{1,2,0:T(8,128)(2,1)}) %all-gather.3.cloned.1.call-update) | async-done | bytes 8847376 | tf_op jit(solution)/shard_map/all_gather | solution.py:50
  169.3 10.0 %mul.49 = bf16[2,768,2880]{1,2,0:T(8,128)(2,1)} multiply(bf16[2,768,2880]{1,2,0:T(8,128)(2,1)} %all-gather.3.cloned.1.call-done, bf16[2,768,2880]{1,2,0:T(8,128)(2,1)} %copy.22) | non-fusion elementwise | flops 4423680 | bytes 26542080 | tf_op jit(solution)/shard_map/mul | solution.py:29
  179.3 0.3 all-reduce.9.cloned.1.call-start
  179.6 0.4 copy-done.9
  179.9 0.6 dynamic-slice
  181.2 4.5 %fusion.16 = f32[2,672,1536]{2,1,0:T(8,128)} fusion(bf16[2,672,64]{1,2,0:T(8,128)(2,1)S(1)} %copy-done.5, bf16[2,1536,64]{1,2,0:T(8,128)(2,1)S(1)} %copy-done.3), kind=kOutput, calls=%fused_computation.33 | convolution fusion | flops 264241152 | bytes 8822784 | tf_op jit(solution)/shard_map/swm,skm->swk/dot_general | solution.py:66
  185.6 73.5 %all-reduce.7.cloned.1.call-done = f32[2,64,2880]{2,1,0:T(8,128)} async-done(((f32[2,64,2880]{2,1,0:T(8,128)}), f32[2,64,2880]{2,1,0:T(8,128)}) %all-reduce.7.cloned.1.call-update) | async-done | bytes 1474576
  259.1 1.7 constant_dynamic-slice_fusion.2
  260.9 64.0 %reduce-scatter.5.cloned.1.call-done = f32[192,128]{1,0:T(8,128)} async-done(((f32[1536,128]{1,0:T(8,128)}), f32[192,128]{1,0:T(8,128)}) %reduce-scatter.5.cloned.1.call-update) | async-done | bytes 98320
  324.8 1.0 reshape.63
  325.9 0.8 copy.24
  326.7 32.4 %all-gather.5.cloned.1.call-done = bf16[2,1536,2880]{1,2,0:T(8,128)(2,1)} async-done(((bf16[2,768,2880]{1,2,0:T(8,128)(2,1)}), bf16[2,1536,2880]{1,2,0:T(8,128)(2,1)}) %all-gather.5.cloned.1.call-update) | async-done | bytes 17694736 | tf_op jit(solution)/shard_map/all_gather | solution.py:57
  359.1 22.6 %multiply_add_fusion = f32[2,672,1536]{2,1,0:T(8,128)} fusion(f32[2,672,1536]{2,1,0:T(8,128)} %fusion.16, bf16[2,1536,2880]{1,2,0:T(8,128)(2,1)} %all-gather.5.cloned.1.call-done, bf16[1,672,2880]{2,1,0:T(8,128)(2,1)} %bitcast.39, bf16[1,672,2880]{2,1,0:T(8,128)(2,1)} %bitcast.36, pred[2,672]{1,0:T(4,128)(4,1)S(1)} %iota_compare_fusion), kind=kOutput, calls=%fused_computation.3 | convolution fusion | flops 11902722048 | bytes 41952576 | tf_op jit(solution)/shard_map/ecd,end->ecn/dot_general | solution.py:54
  381.8 4.5 %slice_bitcast_fusion.1 = f32[672,1536]{1,0:T(8,128)} fusion(f32[2,672,1536]{2,1,0:T(8,128)} %multiply_add_fusion), kind=kLoop, calls=%fused_computation.10 | loop fusion | bytes 8257536 | tf_op jit(solution)/shard_map/squeeze | solution.py:80
  386.3 4.9 %broadcast_in_dim.20 = f32[1568,1536]{1,0:T(8,128)} broadcast(f32[]{:T(128)} %constant.11.clone.1), dimensions={} | broadcast | bytes 9633796 | tf_op jit(solution)/shard_map/broadcast_in_dim | solution.py:76
  391.2 10.9 %dynamic_update_slice.6 = f32[1568,1536]{1,0:T(8,128)} dynamic-update-slice(f32[1568,1536]{1,0:T(8,128)} %broadcast_in_dim.20, f32[672,1536]{1,0:T(8,128)} %slice_bitcast_fusion.1, s32[]{:T(128)S(6)} %select_n.21, s32[]{:T(128)} %constant.13.clone.1) | dynamic-update-slice | bytes 8257540 | tf_op jit(solution)/shard_map/dynamic_update_slice | solution.py:79
  402.1 6.4 %fusion = f32[672,1536]{1,0:T(8,128)} fusion(f32[2,672,1536]{2,1,0:T(8,128)} %multiply_add_fusion, f32[1568,1536]{1,0:T(8,128)} %dynamic_update_slice.6, s32[]{:T(128)S(6)} %select_n.22), kind=kLoop, calls=%fused_computation.9 | loop fusion | flops 1032192 | bytes 12386308 | tf_op jit(solution)/shard_map/add | solution.py:80
  408.6 11.1 %dynamic_update_slice.7 = f32[1568,1536]{1,0:T(8,128)} dynamic-update-slice(f32[1568,1536]{1,0:T(8,128)} %dynamic_update_slice.6, f32[672,1536]{1,0:T(8,128)} %fusion, s32[]{:T(128)S(6)} %select_n.22, s32[]{:T(128)} %constant.13.clone.1) | dynamic-update-slice | bytes 8257540 | tf_op jit(solution)/shard_map/dynamic_update_slice | solution.py:79
  419.7 4.4 %slice.34 = bf16[896,1536]{1,0:T(8,128)(2,1)} slice(f32[1568,1536]{1,0:T(8,128)} %dynamic_update_slice.7), slice={[0:896], [0:1536]} | slice | bytes 5505024 | tf_op jit(solution)/shard_map/slice | solution.py:82
  424.1 1.6 copy.33
  425.7 1.6 copy.34
  (23 shorter events, 0.1 us)
Async XLA Ops:
  7.2 1.6 copy-start
  7.2 162.1 %all-gather.3.cloned.1.call-start = ((), (), s32[]{:S(2)}) async-start(), calls=%async_computation.1 | async-start | bytes 9953280 | tf_op jit(solution)/shard_map/all_gather | solution.py:50
  9.9 249.2 %all-reduce.7.cloned.1.call-start = ((), (), s32[]{:S(2)}) async-start(), calls=%async_computation.4 | async-start | bytes 3014656
  33.0 6.4 %copy-start.7 = (s32[1,2]{1,0:T(1,128)S(1)}, s32[1,2]{1,0:T(1,128)}, u32[]{:S(2)}) copy-start(s32[1,2]{1,0:T(1,128)} %param.11) | copy-start | bytes 28
  39.4 5.9 %copy-start.3 = (bf16[2,1536,64]{1,2,0:T(8,128)(2,1)S(1)}, bf16[2,1536,64]{1,2,0:T(8,128)(2,1)}, u32[]{:S(2)}) copy-start(bf16[2,1536,64]{1,2,0:T(8,128)(2,1)} %param.14) | copy-start | bytes 1179652
  45.3 8.4 %copy-start.8 = (bf16[2,64,2880]{2,1,0:T(8,128)(2,1)S(1)}, bf16[2,64,2880]{2,1,0:T(8,128)(2,1)}, u32[]{:S(2)}) copy-start(bf16[2,64,2880]{2,1,0:T(8,128)(2,1)} %param.15) | copy-start | bytes 2211844
  53.5 271.3 %reduce-scatter.5.cloned.1.call-start = ((), (), s32[]{:S(2)}) async-start(), calls=%async_computation.3 | async-start | bytes 884736
  53.7 6.8 %copy-start.2 = (bf16[1,672,1536]{2,1,0:T(8,128)(2,1)S(1)}, bf16[1,672,1536]{2,1,0:T(8,128)(2,1)}, u32[]{:S(2)}) copy-start(bf16[1,672,1536]{2,1,0:T(8,128)(2,1)} %get-tuple-element.8) | copy-start | bytes 6193156
  59.8 0.7 copy-start.4
  61.5 2.7 copy-start.6
  64.1 295.0 %all-gather.5.cloned.1.call-start = ((), (), s32[]{:S(2)}) async-start(), calls=%async_computation.2 | async-start | bytes 26542080 | tf_op jit(solution)/shard_map/all_gather | solution.py:57
  179.3 0.7 copy-start.9
  179.3 1.9 copy-start.5
  179.3 244.8 %all-reduce.9.cloned.1.call-start = ((), (), s32[]{:S(2)}) async-start(), calls=%async_computation.5 | async-start | bytes 655360 | tf_op jit(solution)/shard_map/psum | solution.py:87
  408.6 18.7 %copy-start.1 = (bf16[2,1536,360]{1,2,0:T(8,128)(2,1)S(1)}, bf16[2,1536,360]{1,2,0:T(8,128)(2,1)}, u32[]{:S(2)}) copy-start(bf16[2,1536,360]{1,2,0:T(8,128)(2,1)} %param.12) | copy-start | bytes 6635524
Sparse Core Ops, SparseCore 0:
  10.3 158.9 all-gather.2
  173.0 86.0 all-reduce.6
  263.4 61.4 reduce-scatter.4
  326.2 32.8 all-gather.4
  361.9 19.5 all-reduce.8
where the time goes:
time: 437 us; the launch traced here: 434 us
  waiting for transfers between devices  211 us (48%)
  local copies, waits for them, and re-layouts  93.8 us (21%)
  blocking collectives  45.8 us (10%)
  matrix products  42.3 us (10%)
  other arithmetic  21.4 us (5%)
  between operations  18.5 us (4%)
    unnamed x7, waiting for transfers between devices  138 us
    all_gather x1, blocking collectives, per_device(): lax.all_gather(own_scales, 'fsdp', axis=2, tiled=True)  45.8 us
    all_gather x1, waiting for transfers between devices, per_device(): lax.all_gather(own_values, 'fsdp', axis=2, tiled=True)  41.4 us
    all_gather x1, waiting for transfers between devices, per_device(): lax.all_gather(half_weights, 'dp', axis=1, tiled=True)  32.4 us
    dot_general x1, matrix products, per_device(): jnp.einsum('ecd,end->ecn', slot_gradients, lax.all_gather(half_weights, '...  22.6 us
    dynamic_update_slice x2, local copies, waits for them, and re-layouts, per_device(): lax.dynamic_update_slice_in_dim(assembled, current + slot_output_rows[exp...  22 us
    dynamic_slice x3, local copies, waits for them, and re-layouts, expert_slices(): lax.dynamic_slice_in_dim(padded, offsets[expert], capacity, 0)  20.1 us
    mul x2, local copies, waits for them, and re-layouts, dequantize(): shaped * block_scales[:, :, None, :]  16 us
  transfers between devices with their start and end apart: 5, of which 4 were waited for; matrix products, arithmetic and copies ran while one was open for 35% of the time, Pallas kernels for 0%

commit v1 on v0

--- a/solution.py
+++ b/solution.py
@@ -1,6 +1,10 @@
+import functools
+
 import jax
 import jax.numpy as jnp
 from jax import lax
+from jax.experimental import pallas as pl
+from jax.experimental.pallas import tpu as pltpu
 from jax.sharding import PartitionSpec as P
 
 HIDDEN_UNITS = 1536
@@ -88,6 +92,288 @@
     return (grad_hidden, grad_a, grad_b)
 
 
+def fits(mesh, output_gradient, hidden, values):
+    peers = mesh.shape["fsdp"]
+    rows = output_gradient.shape[0] // (peers * mesh.shape["dp"] * mesh.shape["groups"])
+    wide = lane_padded(values.shape[2] // peers)
+    total = 2 * (peers + 1) * values.shape[0] * values.shape[1] * wide
+    total += 2 * peers * EXPERTS_ACTIVE * CAP * wide + rows * hidden.shape[1] * 8
+    return (
+        mesh.shape["groups"] == 2
+        and mesh.shape["dp"] == 2
+        and peers % 2 == 0
+        and peers > 2
+        and total < 44 * 2**20
+    )
+
+
+def lane_padded(size):
+    return -(-size // 128) * 128
+
+
+def ring_kernel(
+    peers, own_ref, gated_ref, low_ref, maps_ref, terms_ref, hidden_out, terms_out,
+    weights, total, sums_in, sums, sums_low, sums_got, final,
+    send_right, recv_right, send_left, recv_left, send_pair, recv_pair, send_core, recv_core,
+    send_half, recv_half, send_sum, recv_sum, send_final, recv_final,
+):
+    group, core, me = lax.axis_index("groups"), lax.axis_index("dp"), lax.axis_index("fsdp")
+    last = 2 * (peers - 1)
+    skip = total.shape[1] - CAP
+
+    def place(position):
+        return jnp.where(position < peers // 2, 2 * position, 2 * (peers - 1 - position) + 1)
+
+    position = jnp.where(lax.rem(me, 2) == 0, me // 2, peers - 1 - me // 2)
+    right = {"fsdp": place(lax.rem(position + 1, peers))}
+    left = {"fsdp": place(lax.rem(position + peers - 1, peers))}
+    pair, sibling = {"groups": 1 - group}, {"dp": 1 - core}
+    mesh_id = pl.DeviceIdType.MESH
+
+    barrier = pltpu.get_barrier_semaphore()
+    for offset in range(1, peers):
+        pl.semaphore_signal(
+            barrier, inc=1, device_id={"fsdp": lax.rem(me + offset, peers)}, device_id_type=mesh_id
+        )
+    pl.semaphore_signal(barrier, inc=1, device_id=pair, device_id_type=mesh_id)
+    pl.semaphore_signal(barrier, inc=1, device_id=sibling, device_id_type=mesh_id)
+    pl.semaphore_wait(barrier, peers + 1)
+
+    def remote(source, target, send_sem, recv_sem, device):
+        return pltpu.make_async_remote_copy(
+            src_ref=source, dst_ref=target, send_sem=send_sem, recv_sem=recv_sem,
+            device_id=device, device_id_type=mesh_id,
+        )
+
+    third_right, third_left, third_pair = 2 * group, 1, 2 - 2 * group
+    mine, others = 3 * core, 3 - 3 * core
+
+    def owner_right(k):
+        return place(lax.rem(position + peers - (k // 2 + 1), peers))
+
+    def owner_left(k):
+        return place(lax.rem(position + k // 2 + 1, peers))
+
+    def right_copy(source, owner, k):
+        target = weights.at[owner, mine + third_right, lax.rem(k, 2)]
+        return remote(target if source is None else source, target, send_right.at[k], recv_right.at[k], right)
+
+    def left_copy(source, owner, k):
+        target = weights.at[owner, mine + third_left, lax.rem(k, 2)]
+        return remote(target if source is None else source, target, send_left.at[k], recv_left.at[k], left)
+
+    def pair_copy(k, third):
+        block = weights.at[owner_right(k), mine + third, lax.rem(k, 2)]
+        return remote(block, block, send_pair.at[k], recv_pair.at[k], pair)
+
+    def core_copy(kind, k, base):
+        owner = owner_left(k) if kind == 1 else owner_right(k)
+        third = (third_right, third_left, third_pair)[kind]
+        block = weights.at[owner, base + third, lax.rem(k, 2)]
+        return remote(block, block, send_core.at[kind, k], recv_core.at[kind, k], sibling)
+
+    for k in range(2):
+        right_copy(own_ref.at[mine + third_right, k], me, k).start()
+        left_copy(own_ref.at[mine + third_left, k], me, k).start()
+    half_copy = remote(terms_ref.at[1 - core], sums_in, send_half, recv_half, sibling)
+    half_copy.start()
+
+    def sum_copy(offset):
+        return remote(
+            sums_low.at[lax.rem(me + offset, peers)], sums_got.at[offset - 1],
+            send_sum.at[offset - 1], recv_sum.at[offset - 1], {"fsdp": lax.rem(me + offset, peers)},
+        )
+
+    def final_copy(which):
+        return remote(final.at[which], final.at[which], send_final, recv_final, sibling)
+
+    contract = (((1,), (1,)), ((), ()))
+
+    def prepare(part, carry):
+        total[part] = adapter_scale * lax.dot_general(
+            low_ref[...], maps_ref[part], contract, preferred_element_type=jnp.float32
+        )
+        return carry
+
+    lax.fori_loop(0, 6, prepare, 0)
+
+    def add_product(block, owner, expert, part):
+        rows = pl.ds(pl.multiple_of(expert * skip, 32), CAP)
+        total[part, rows, :] += lax.dot_general(
+            gated_ref[expert, owner], block, contract, preferred_element_type=jnp.float32
+        )
+
+    def step(k, carry):
+        @pl.when(k < last)
+        def _():
+            right_copy(None, owner_right(k), k).wait_recv()
+
+            @pl.when(k < last - 2)
+            def _():
+                right_copy(None, owner_right(k), k + 2).start()
+
+            pair_copy(k, third_right).start()
+            core_copy(0, k, mine).start()
+            left_copy(None, owner_left(k), k).wait_recv()
+
+            @pl.when(k < last - 2)
+            def _():
+                left_copy(None, owner_left(k), k + 2).start()
+
+            core_copy(1, k, mine).start()
+
+        @pl.when(k < 12)
+        def _():
+            add_product(own_ref[k // 2, lax.rem(k, 2)], me, lax.rem(k, 2), k // 2)
+
+        @pl.when(k == 2)
+        def _():
+            half_copy.wait_recv()
+
+            def add_half(block, carry):
+                sums[block] = terms_ref[core, block] + sums_in[block]
+                sums_low[block] = sums[block].astype(jnp.bfloat16)
+                return carry
+
+            lax.fori_loop(0, peers, add_half, 0)
+            for offset in range(1, peers):
+                sum_copy(offset).start()
+
+        @pl.when(k == last - 3)
+        def _():
+            summed = sums[me]
+            for offset in range(1, peers):
+                sum_copy(offset).wait_recv()
+                summed = summed + sums_got[offset - 1].astype(jnp.float32)
+            final[core] = summed
+            final_copy(core).start()
+
+        @pl.when((k >= 1) & (k < last + 1))
+        def _():
+            now = k - 1
+            expert = lax.rem(now, 2)
+            pair_copy(now, third_pair).wait_recv()
+            core_copy(2, now, mine).start()
+            core_copy(0, now, others).wait_recv()
+            core_copy(1, now, others).wait_recv()
+            first, second = owner_right(now), owner_left(now)
+            for base in (mine, others):
+                part = base + third_right
+                add_product(weights[first, part, expert], first, expert, part)
+                part = base + third_left
+                add_product(weights[second, part, expert], second, expert, part)
+
+        @pl.when(k >= 2)
+        def _():
+            now = k - 2
+            expert = lax.rem(now, 2)
+            core_copy(2, now, others).wait_recv()
+            owner = owner_right(now)
+            for base in (mine, others):
+                part = base + third_pair
+                add_product(weights[owner, part, expert], owner, expert, part)
+
+        return carry
+
+    lax.fori_loop(0, last + 2, step, 0)
+
+    for part in range(6):
+        width = total.shape[2]
+        hidden_out[:, part * width:(part + 1) * width] = total[part].astype(jnp.bfloat16)
+    final_copy(1 - core).wait_recv()
+    terms_out[...] = final[...]
+
+    def finish(k, carry):
+        right_copy(None, me, k).wait_send()
+        left_copy(None, me, k).wait_send()
+        pair_copy(k, third_right).wait_send()
+        for kind in range(3):
+            core_copy(kind, k, mine).wait_send()
+        return carry
+
+    lax.fori_loop(0, last, finish, 0)
+    half_copy.wait_send()
+    final_copy(core).wait_send()
+    for offset in range(1, peers):
+        sum_copy(offset).wait_send()
+
+
+def per_device_ring(
+    output_gradient, hidden, gates, counts, values, scales, adapter_input_maps, adapter_output_maps
+):
+    peers = lax.axis_size("fsdp")
+    rows, width = output_gradient.shape
+    units, rank = hidden.shape[1], adapter_input_maps.shape[2]
+    columns = width // peers
+    wide = lane_padded(columns)
+    split = counts[0, 0]
+    pad = ((0, 0), (0, 0), (0, wide - columns))
+    own = jnp.pad(dequantize(values, scales), pad)
+    own = own.reshape(EXPERTS_ACTIVE, 6, units // 6, wide).transpose(1, 0, 2, 3)
+    gated = (gates[:, None] * output_gradient.astype(jnp.float32)).astype(jnp.bfloat16)
+    blocks = jnp.pad(gated.reshape(rows, peers, columns), pad).transpose(1, 0, 2)
+    row_ids = lax.broadcasted_iota(jnp.int32, (rows, 1), 0)
+    first = row_ids < split
+    zero = jnp.zeros((), jnp.bfloat16)
+    masked = jnp.stack(
+        [
+            jnp.where(first[None, :CAP], blocks[:, :CAP], zero),
+            jnp.where(first[None, rows - CAP:], zero, blocks[:, rows - CAP:]),
+        ]
+    )
+    maps_in = jnp.concatenate([adapter_input_maps[0], adapter_input_maps[1]], axis=1)
+    maps_out = adapter_output_maps.reshape(EXPERTS_ACTIVE * rank, width)
+    of_expert = first == (lax.broadcasted_iota(jnp.int32, (1, EXPERTS_ACTIVE * rank), 1) < rank)
+    low_in = jnp.dot(hidden, maps_in, preferred_element_type=jnp.float32)
+    low_in = jnp.where(of_expert, low_in, 0.0).astype(jnp.bfloat16)
+    low_back = jnp.einsum("rd,kd->rk", gated, maps_out, preferred_element_type=jnp.float32)
+    low_back = jnp.where(of_expert, low_back, 0.0).astype(jnp.bfloat16)
+    term_a = jnp.einsum("rh,rk->hk", hidden, low_back, preferred_element_type=jnp.float32)
+    term_b = jnp.einsum("jrd,rk->jdk", blocks, low_in, preferred_element_type=jnp.float32)
+    terms = jnp.concatenate([term_a.reshape(peers, units // peers, -1), term_b], axis=1)
+    tall = terms.shape[1]
+    terms = terms.reshape(peers, 2, tall // 2, 2 * rank).transpose(1, 0, 2, 3)
+    maps_parts = maps_in.reshape(6, units // 6, 2 * rank)
+    last = 2 * (peers - 1)
+    half = (tall // 2, 2 * rank)
+    dma = pltpu.SemaphoreType.DMA
+    vmem = pl.BlockSpec(memory_space=pltpu.VMEM)
+    grad_hidden, summed = pl.pallas_call(
+        functools.partial(ring_kernel, peers),
+        out_shape=(
+            jax.ShapeDtypeStruct((rows, units), jnp.bfloat16),
+            jax.ShapeDtypeStruct((2,) + half, jnp.float32),
+        ),
+        in_specs=[vmem] * 5,
+        out_specs=(vmem, vmem),
+        scratch_shapes=[
+            pltpu.VMEM((peers,) + own.shape, jnp.bfloat16),
+            pltpu.VMEM((6, rows, units // 6), jnp.float32),
+            pltpu.VMEM((peers,) + half, jnp.float32),
+            pltpu.VMEM((peers,) + half, jnp.float32),
+            pltpu.VMEM((peers,) + half, jnp.bfloat16),
+            pltpu.VMEM((peers - 1,) + half, jnp.bfloat16),
+            pltpu.VMEM((2,) + half, jnp.float32),
+        ]
+        + [dma((last,))] * 6
+        + [dma((3, last))] * 2
+        + [dma, dma]
+        + [dma((peers - 1,))] * 2
+        + [dma, dma],
+        compiler_params=pltpu.CompilerParams(
+            collective_id=0, has_side_effects=True, vmem_limit_bytes=58 * 2**20
+        ),
+        cost_estimate=pl.CostEstimate(
+            flops=2 * EXPERTS_ACTIVE * CAP * width * units, bytes_accessed=20 * 2**20, transcendentals=0
+        ),
+    )(own, masked, low_back, maps_parts, terms)
+    summed = adapter_scale * summed.reshape(tall, EXPERTS_ACTIVE, rank)
+    cut = units // peers
+    grad_a = summed[:cut].transpose(1, 0, 2)
+    grad_b = summed[cut:cut + columns].transpose(1, 2, 0)
+    return grad_hidden, grad_a, grad_b
+
+
 def solution(mesh):
     placed = (
         P(("groups", "dp", "fsdp"), None),
@@ -99,14 +385,19 @@
         P("groups", None, None),
         P("groups", None, None),
     )
-    return jax.shard_map(
-        per_device,
-        mesh=mesh,
-        in_specs=placed,
-        out_specs=(
-            P(("groups", "dp", "fsdp"), None),
-            P("groups", "fsdp", None),
-            P("groups", None, "fsdp"),
-        ),
-        check_vma=False,
-    )
+
+    def whole(output_gradient, hidden, gates, counts, values, *rest):
+        ring = fits(mesh, output_gradient, hidden, values)
+        return jax.shard_map(
+            per_device_ring if ring else per_device,
+            mesh=mesh,
+            in_specs=placed,
+            out_specs=(
+                P(("groups", "dp", "fsdp"), None),
+                P("groups", "fsdp", None),
+                P("groups", None, "fsdp"),
+            ),
+            check_vma=False,
+        )(output_gradient, hidden, gates, counts, values, *rest)
+
+    return whole

time: 437 us -> 158 us (0.36)
  waiting for transfers between devices: 211 us -> 0 us
  Pallas kernels: 0 us -> 93.5 us
  local copies, waits for them, and re-layouts: 93.8 us -> 27.5 us
  blocking collectives: 45.8 us -> 0 us
  matrix products: 42.3 us -> 13.1 us
  between operations: 18.5 us -> 0.77 us
    unnamed x7 -> x0, waiting for transfers between devices: 138 us -> none
    pallas_call x0 -> x1, Pallas kernels: none -> 93.5 us  [per_device_ring(): pl.pallas_call(functools.partial(ring_kernel, peers), out_shape=(jax.Shap...]
    all_gather x2 -> x0, waiting for transfers between devices: 73.9 us -> none  [the longest x1 41.4 us: per_device(): lax.all_gather(own_values, 'fsdp', axis=2, tiled=True)]
    all_gather x1 -> x0, blocking collectives: 45.8 us -> none  [per_device(): lax.all_gather(own_scales, 'fsdp', axis=2, tiled=True)]
    dot_general x5 -> x3, matrix products: 42.3 us -> 13.1 us  [the longest x1 7.37 us: per_device_ring(): jnp.einsum('jrd,rk->jdk', blocks, low_in, preferred_element_type=jnp.floa...]
    dynamic_update_slice x2 -> x0, local copies, waits for them, and re-layouts: 22 us -> none  [per_device(): lax.dynamic_update_slice_in_dim(assembled, current + slot_output_rows[exp...]
    dynamic_slice x5 -> x0, local copies, waits for them, and re-layouts: 21.1 us -> none  [the longest x3 20.1 us: expert_slices(): lax.dynamic_slice_in_dim(padded, offsets[expert], capacity, 0)]
    mul x2, local copies, waits for them, and re-layouts: 16 us -> 0.46 us  [per_device_ring(): summed = adapter_scale * summed.reshape(tall, EXPERTS_ACTIVE, rank)]
  transfers between devices with their start and end apart: 5 -> 0, of which waited for: 4 -> 0; matrix products, arithmetic and copies ran while one was open for 35% -> 0% of each run, Pallas kernels for 0% -> 0%
where the time goes in v1:
time: 158 us
  Pallas kernels  93.5 us (59%)
  local copies, waits for them, and re-layouts  27.5 us (17%)
  other arithmetic  22.8 us (14%)
  matrix products  13.1 us (8%)
    pallas_call x1, Pallas kernels, per_device_ring(): pl.pallas_call(functools.partial(ring_kernel, peers), out_shape=(jax.Shap...  93.5 us
    another operation x2, other arithmetic, per_device_ring(): jnp.stack([jnp.where(first[None, :CAP], blocks[:, :CAP], zero), jnp.where...  11.5 us
    reshape x1, local copies, waits for them, and re-layouts, per_device_ring(): gated.reshape(rows, peers, columns)  8.27 us
    dot_general x1, matrix products, per_device_ring(): jnp.einsum('jrd,rk->jdk', blocks, low_in, preferred_element_type=jnp.floa...  7.37 us
    unnamed x18, local copies, waits for them, and re-layouts  6.62 us
    convert_element_type x1, other arithmetic, per_device_ring(): (gates[:, None] * output_gradient.astype(jnp.float32)).astype(jnp.bfloat16)  5.8 us
    dot_general x1, matrix products, per_device_ring(): jnp.einsum('rd,kd->rk', gated, maps_out, preferred_element_type=jnp.float32)  4.24 us
    transpose x1, local copies, waits for them, and re-layouts, per_device_ring(): jnp.pad(gated.reshape(rows, peers, columns), pad).transpose(1, 0, 2)  3.2 us

profile of v1, /device:TPU:16, one launch (start us, length us, event | category | flops | bytes accessed | tf_op | source)
XLA Modules:
  0.0 157.7 jit_solution(12200232619525339136)
XLA Ops:
  0.6 0.0 copy-start
  0.6 2.0 %slice_bitcast_fusion.3 = (bf16[1536,64]{0,1:T(8,128)(2,1)S(1)}, bf16[1536,64]{0,1:T(8,128)(2,1)S(1)}, bf16[1,1536,64]{1,2,0:T(8,128)(2,1)}, bf16[1,1536,64]{1,2,0:T(8,128)(2,1)}) fusion(bf16[2,1536,64]{1,2,0:T(8,128)(2,1)} %param.14), kind=kLoop, calls=%fused_computation.38 | loop fusion | bytes 1179648 | tf_op jit(solution)/shard_map/squeeze | solution.py:324
  2.6 5.8 %multiply_convert_fusion = bf16[896,2880]{0,1:T(8,128)(2,1)} fusion(bf16[896,2880]{0,1:T(8,128)(2,1)} %param.8, f32[896]{0:T(1024)} %param.10), kind=kLoop, calls=%fused_computation | loop fusion | flops 7741440 | bytes 10325504 | tf_op jit(solution)/shard_map/convert_element_type | solution.py:313
  8.4 0.0 copy-start.7
  8.4 8.3 %copy.20 = bf16[896,8,360]{2,0,1:T(8,128)(2,1)} copy(bf16[896,8,360]{0,2,1:T(8,128)(2,1)} %bitcast.55) | data formatting | bytes 10321920 | tf_op jit(solution)/shard_map/reshape | solution.py:314
  16.7 0.0 copy-done.7
  16.8 0.0 copy-done
  16.8 7.4 %fusion.6 = f32[8,384,128]{2,1,0:T(8,128)} fusion(bf16[896,1536]{1,0:T(8,128)(2,1)S(1)} %copy-done, bf16[1536,64]{0,1:T(8,128)(2,1)S(1)} %get-tuple-element.12, bf16[1536,64]{0,1:T(8,128)(2,1)S(1)} %get-tuple-element.11, pred[128]{0:T(512)(128)(4,1)S(1)} %iota_compare_fusion.2, pred[896]{0:T(1024)(128)(4,1)S(1)} %iota_compare_fusion, ...), kind=kOutput, calls=%fused_computation.18 | convolution fusion | flops 1058095104 | bytes 9880576 | tf_op jit(solution)/shard_map/jrd,rk->jdk/dot_general | solution.py:332
  24.1 4.2 %fusion.4.low_ref = bf16[896,128]{1,0:T(8,128)(2,1)S(1)} fusion(bf16[896,2880]{0,1:T(8,128)(2,1)} %multiply_convert_fusion, bf16[128,2880]{1,0:T(8,128)(2,1)} %bitcast.65, pred[128]{0:T(512)(128)(4,1)S(1)} %iota_compare_fusion.2, pred[896]{0:T(1024)(128)(4,1)S(1)} %iota_compare_fusion), kind=kOutput, calls=%fused_computation.16 | convolution fusion | flops 660946944 | bytes 6128640 | tf_op jit(solution)/shard_map/rd,kd->rk/dot_general | solution.py:329
  28.4 0.0 copy-start.5
  28.4 0.7 copy-done.5
  29.1 1.5 convolution_bitcast_fusion
  30.6 1.4 copy.23
  32.0 1.6 %pad_maximum_fusion.1 = f32[8,576,128]{2,1,0:T(8,128)S(1)} fusion(f32[8,384,128]{2,1,0:T(8,128)} %fusion.6, f32[8,192,128]{2,1,0:T(8,128)S(1)} %bitcast.58), kind=kLoop, calls=%fused_computation.8 | loop fusion | flops 589824 | bytes 4718592 | tf_op jit(solution)/shard_map/concatenate | solution.py:333
  33.5 1.6 %copy.30 = f32[8,2,288,128]{3,2,0,1:T(8,128)} copy(f32[8,2,288,128]{3,2,1,0:T(8,128)S(1)} %bitcast.56) | data formatting | bytes 4718592 | tf_op jit(solution)/shard_map/reshape | solution.py:335
  35.1 3.2 %pad_bitcast_fusion = bf16[8,896,384]{2,1,0:T(8,128)(2,1)S(1)} fusion(bf16[896,8,360]{2,0,1:T(8,128)(2,1)} %copy.20), kind=kLoop, calls=%fused_computation.2 | loop fusion | bytes 10665984 | tf_op jit(solution)/shard_map/transpose | solution.py:314
  38.4 0.1 slice_reduce_fusion.1
  38.5 3.8 %fusion.1 = (bf16[1,8,672,384]{3,2,1,0:T(8,128)(2,1)}, bf16[1,8,672,384]{3,2,1,0:T(8,128)(2,1)}) fusion(bf16[8,896,384]{2,1,0:T(8,128)(2,1)S(1)} %pad_bitcast_fusion, pred[672]{0:T(1024)(128)(4,1)S(1)} %get-tuple-element.7, pred[672]{0:T(1024)(128)(4,1)S(1)} %get-tuple-element.8), kind=kLoop, calls=%fused_computation.6 | loop fusion | flops 4128768 | bytes 16516416 | tf_op jit(solution)/shard_map/stack | solution.py:318
  42.3 0.0 copy-start.4
  42.3 0.0 copy-start.3
  42.3 0.0 copy-start.2
  42.3 7.7 %pad_maximum_fusion.gated_ref = bf16[2,8,672,384]{3,2,1,0:T(8,128)(2,1)} fusion(bf16[1,8,672,384]{3,2,1,0:T(8,128)(2,1)} %get-tuple-element.10, bf16[1,8,672,384]{3,2,1,0:T(8,128)(2,1)} %get-tuple-element.9), kind=kLoop, calls=%fused_computation.1 | loop fusion | flops 4128768 | bytes 16515072 | tf_op jit(solution)/shard_map/stack | solution.py:318
  49.9 0.0 copy-start.6
  49.9 0.0 copy-done.4
  50.0 0.2 copy.22
  50.2 0.0 copy-done.3
  50.2 0.2 copy.21
  50.4 1.0 pad_maximum_fusion.2.maps_ref
  51.4 0.0 copy-done.2
  51.4 2.4 %copy.18 = bf16[2,1536,360]{2,1,0:T(8,128)(2,1)} copy(bf16[2,1536,360]{1,2,0:T(8,128)(2,1)S(1)} %copy-done.2) | data formatting | bytes 4423680 | tf_op args[4]
  53.8 0.0 copy-done.6
  53.8 1.9 %bitcast_multiply_fusion = bf16[2,1536,360]{2,1,0:T(8,128)(2,1)S(1)} fusion(bf16[2,1536,360]{2,1,0:T(8,128)(2,1)} %copy.18, bf16[2,48,360]{2,1,0:T(8,128)(2,1)S(1)} %copy-done.6), kind=kLoop, calls=%fused_computation.9 | loop fusion | flops 1105920 | bytes 4492800 | tf_op jit(solution)/shard_map/mul | solution.py:33
  55.8 0.3 pad.8
  56.1 1.7 %copy.31 = bf16[2,6,256,384]{3,2,0,1:T(8,128)(2,1)} copy(bf16[2,6,256,384]{3,2,1,0:T(8,128)(2,1)S(1)} %bitcast.57) | data formatting | bytes 4718592 | tf_op jit(solution)/shard_map/reshape | solution.py:312
  57.8 0.0 copy-start.1
  57.8 93.5 %shard_map.103 = (bf16[896,1536]{1,0:T(8,128)(2,1)}, f32[2,288,128]{2,1,0:T(8,128)}) custom-call(bf16[6,2,256,384]{3,2,1,0:T(8,128)(2,1)} %bitcast.60, bf16[2,8,672,384]{3,2,1,0:T(8,128)(2,1)} %pad_maximum_fusion.gated_ref, bf16[896,128]{1,0:T(8,128)(2,1)} %copy-done.5, bf16[6,256,128]{2,1,0:T(8,128)(2,1)} %pad_maximum_fusion.2.maps_ref, ...), custom_call_target="tpu_custom_call" | custom-call | flops 11890851840 | bytes 20971520 | tf_op jit(solution)/shard_map/pallas_call | solution.py:341
  151.3 1.0 broadcast_multiply_fusion
  152.3 0.2 copy.26
  152.5 0.3 mul.35
  152.8 0.8 slice_bitcast_fusion
  153.6 0.7 slice_bitcast_fusion.1
  154.2 3.5 %copy.33 = bf16[896,1536]{1,0:T(8,128)(2,1)} copy(bf16[896,1536]{1,0:T(8,128)(2,1)} %get-tuple-element.18) | data formatting | bytes 5505024
  157.7 0.0 copy-done.1
  (3 shorter events, 0.1 us)
Async XLA Ops:
  0.6 16.1 %copy-start = (bf16[896,1536]{1,0:T(8,128)(2,1)S(1)}, bf16[896,1536]{1,0:T(8,128)(2,1)}, u32[]{:S(2)}) copy-start(bf16[896,1536]{1,0:T(8,128)(2,1)} %param.9) | copy-start | bytes 8257540
  8.4 8.3 %copy-start.7 = (s32[1,2]{1,0:T(1,128)S(1)}, s32[1,2]{1,0:T(1,128)}, u32[]{:S(2)}) copy-start(s32[1,2]{1,0:T(1,128)} %param.11) | copy-start | bytes 28
  28.4 0.7 copy-start.5
  42.3 7.7 %copy-start.4 = (bf16[1,1536,64]{1,2,0:T(8,128)(2,1)S(1)}, bf16[1,1536,64]{1,2,0:T(8,128)(2,1)}, u32[]{:S(2)}) copy-start(bf16[1,1536,64]{1,2,0:T(8,128)(2,1)} %get-tuple-element.13) | copy-start | bytes 589828
  42.3 7.9 %copy-start.3 = (bf16[1,1536,64]{1,2,0:T(8,128)(2,1)S(1)}, bf16[1,1536,64]{1,2,0:T(8,128)(2,1)}, u32[]{:S(2)}) copy-start(bf16[1,1536,64]{1,2,0:T(8,128)(2,1)} %get-tuple-element.14) | copy-start | bytes 589828
  42.3 9.1 %copy-start.2 = (bf16[2,1536,360]{1,2,0:T(8,128)(2,1)S(1)}, bf16[2,1536,360]{1,2,0:T(8,128)(2,1)}, u32[]{:S(2)}) copy-start(bf16[2,1536,360]{1,2,0:T(8,128)(2,1)} %param.12) | copy-start | bytes 6635524
  49.9 3.9 %copy-start.6 = (bf16[2,48,360]{2,1,0:T(8,128)(2,1)S(1)}, bf16[2,48,360]{2,1,0:T(8,128)(2,1)}, u32[]{:S(2)}) copy-start(bf16[2,48,360]{2,1,0:T(8,128)(2,1)} %param.13) | copy-start | bytes 207364
  57.8 100.0 %copy-start.1 = (bf16[896,1536]{1,0:T(8,128)(2,1)S(1)}, bf16[896,1536]{1,0:T(8,128)(2,1)}, u32[]{:S(2)}) copy-start(bf16[896,1536]{1,0:T(8,128)(2,1)} %param.9) | copy-start | bytes 8257540

commit v2 on v1

--- a/solution.py
+++ b/solution.py
@@ -112,10 +112,12 @@
 
 
 def ring_kernel(
-    peers, own_ref, gated_ref, low_ref, maps_ref, terms_ref, hidden_out, terms_out,
-    weights, total, sums_in, sums, sums_low, sums_got, final,
+    peers, columns, gradient_hbm, hidden_hbm, gates_ref, values_ref, scales_ref, maps_ref, back_maps_ref,
+    hidden_out, terms_out,
+    gradient_ref, hidden_ref, own_ref, gated_ref, low_ref, low_in_ref, terms_ref,
+    weights, total, sums, sums_low, sums_got, final,
     send_right, recv_right, send_left, recv_left, send_pair, recv_pair, send_core, recv_core,
-    send_half, recv_half, send_sum, recv_sum, send_final, recv_final,
+    send_half, recv_half, send_sum, recv_sum, send_final, recv_final, load_sem,
 ):
     group, core, me = lax.axis_index("groups"), lax.axis_index("dp"), lax.axis_index("fsdp")
     last = 2 * (peers - 1)
@@ -130,6 +132,27 @@
     pair, sibling = {"groups": 1 - group}, {"dp": 1 - core}
     mesh_id = pl.DeviceIdType.MESH
 
+    third_right, third_left, third_pair = 2 * group, 1, 2 - 2 * group
+    mine, others = 3 * core, 3 - 3 * core
+    depth, wide = own_ref.shape[2:]
+
+    def scale_piece(expert, part):
+        scale = scales_ref[expert, part].astype(jnp.float32)
+        scale = jnp.broadcast_to(scale[:, None, :], (scale.shape[0], depth // scale.shape[0], columns))
+        piece = values_ref[expert, part].astype(jnp.float32) * scale.reshape(depth, columns)
+        own_ref[part, expert, :, :columns] = piece.astype(jnp.bfloat16)
+        own_ref[part, expert, :, columns:] = jnp.zeros((depth, wide - columns), jnp.bfloat16)
+
+    def scale_sent(expert, carry):
+        scale_piece(expert, mine + third_right)
+        scale_piece(expert, mine + third_left)
+        return carry
+
+    load_gradient = pltpu.make_async_copy(gradient_hbm, gradient_ref, load_sem.at[0])
+    load_hidden = pltpu.make_async_copy(hidden_hbm, hidden_ref, load_sem.at[1])
+    load_gradient.start()
+    load_hidden.start()
+    lax.fori_loop(0, 2, scale_sent, 0)
     barrier = pltpu.get_barrier_semaphore()
     for offset in range(1, peers):
         pl.semaphore_signal(
@@ -144,9 +167,6 @@
             src_ref=source, dst_ref=target, send_sem=send_sem, recv_sem=recv_sem,
             device_id=device, device_id_type=mesh_id,
         )
-
-    third_right, third_left, third_pair = 2 * group, 1, 2 - 2 * group
-    mine, others = 3 * core, 3 - 3 * core
 
     def owner_right(k):
         return place(lax.rem(position + peers - (k // 2 + 1), peers))
@@ -175,8 +195,7 @@
     for k in range(2):
         right_copy(own_ref.at[mine + third_right, k], me, k).start()
         left_copy(own_ref.at[mine + third_left, k], me, k).start()
-    half_copy = remote(terms_ref.at[1 - core], sums_in, send_half, recv_half, sibling)
-    half_copy.start()
+    half_copy = remote(terms_ref.at[1 - core], sums, send_half, recv_half, sibling)
 
     def sum_copy(offset):
         return remote(
@@ -189,21 +208,7 @@
 
     contract = (((1,), (1,)), ((), ()))
 
-    def prepare(part, carry):
-        total[part] = adapter_scale * lax.dot_general(
-            low_ref[...], maps_ref[part], contract, preferred_element_type=jnp.float32
-        )
-        return carry
-
-    lax.fori_loop(0, 6, prepare, 0)
-
-    def add_product(block, owner, expert, part):
-        rows = pl.ds(pl.multiple_of(expert * skip, 32), CAP)
-        total[part, rows, :] += lax.dot_general(
-            gated_ref[expert, owner], block, contract, preferred_element_type=jnp.float32
-        )
-
-    def step(k, carry):
+    def comm(k):
         @pl.when(k < last)
         def _():
             right_copy(None, owner_right(k), k).wait_recv()
@@ -222,16 +227,112 @@
 
             core_copy(1, k, mine).start()
 
+        @pl.when((k >= 1) & (k <= last))
+        def _():
+            pair_copy(k - 1, third_pair).wait_recv()
+            core_copy(2, k - 1, mine).start()
+
+    def scale_rest(k, carry):
+        part = jnp.where(k == 0, mine + third_pair, others + jnp.maximum(k - 1, 0))
+        scale_piece(0, part)
+        scale_piece(1, part)
+        return carry
+
+    def expert_rows(expert):
+        return pl.ds(pl.multiple_of(expert * skip, 32), CAP)
+
+    def gate_block(block):
+        window = slice(block * columns, (block + 1) * columns)
+
+        def gate_rows(k, carry):
+            expert, chunk = k // 3, lax.rem(k, 3)
+            rows = pl.ds(pl.multiple_of((expert + chunk) * skip, 32), skip)
+            target = pl.ds(pl.multiple_of(chunk * skip, 32), skip)
+            gated = gradient_ref[rows, window].astype(jnp.float32) * gates_ref[expert, rows, :]
+            gated_ref[expert, block, target, :columns] = gated.astype(jnp.bfloat16)
+            gated_ref[expert, block, target, columns:] = jnp.zeros((skip, wide - columns), jnp.bfloat16)
+            return carry
+
+        lax.fori_loop(0, 6, gate_rows, 0)
+
+    def low_rank(expert, carry):
+        rows = expert_rows(expert)
+        low = jnp.zeros(low_in_ref.shape[1:], jnp.float32)
+        for part in range(6):
+            low += jnp.dot(
+                hidden_ref[rows, part * depth:(part + 1) * depth], maps_ref[expert, part],
+                preferred_element_type=jnp.float32,
+            )
+        low_in_ref[expert] = low.astype(jnp.bfloat16)
+        back = jnp.zeros(low_ref.shape[1:], jnp.float32)
+        for block in range(peers):
+            back += lax.dot_general(
+                gated_ref[expert, block, :, :columns],
+                back_maps_ref[expert, :, block * columns:(block + 1) * columns],
+                contract, preferred_element_type=jnp.float32,
+            )
+        low_ref[expert] = back.astype(jnp.bfloat16)
+        return carry
+
+    def prepare(part, carry):
+        total[part] = jnp.zeros(total.shape[1:], jnp.float32)
+        for expert in range(EXPERTS_ACTIVE):
+            total[part, expert_rows(expert), :] += adapter_scale * lax.dot_general(
+                low_ref[expert], maps_ref[expert, part], contract, preferred_element_type=jnp.float32
+            )
+        return carry
+
+    def outer(low, rows):
+        return lax.dot_general(
+            low, rows, (((0,), (0,)), ((), ())), preferred_element_type=jnp.float32
+        )
+
+    def make_terms(expert, carry):
+        cut = hidden_ref.shape[1] // peers
+        for block in range(peers):
+            terms_ref[expert, block, :, :wide] = outer(low_in_ref[expert], gated_ref[expert, block])
+            terms_ref[expert, block, :, wide:wide + cut] = outer(
+                low_ref[expert], hidden_ref[expert_rows(expert), block * cut:(block + 1) * cut]
+            )
+            terms_ref[expert, block, :, wide + cut:] = jnp.zeros(
+                (terms_ref.shape[2], terms_ref.shape[3] - wide - cut), jnp.float32
+            )
+        return carry
+
+    load_gradient.wait()
+    for block in range(peers // 2):
+        gate_block(block)
+    comm(0)
+    for block in range(peers // 2, peers):
+        gate_block(block)
+    comm(1)
+    lax.fori_loop(0, 4, scale_rest, 0)
+    load_hidden.wait()
+    lax.fori_loop(0, 2, low_rank, 0)
+    comm(2)
+    lax.fori_loop(0, 2, make_terms, 0)
+    half_copy.start()
+    comm(3)
+    lax.fori_loop(0, 6, prepare, 0)
+
+    def add_product(block, owner, expert, part):
+        total[part, expert_rows(expert), :] += lax.dot_general(
+            gated_ref[expert, owner], block, contract, preferred_element_type=jnp.float32
+        )
+
+    def step(k, carry):
+        comm(k + 4)
+
         @pl.when(k < 12)
         def _():
             add_product(own_ref[k // 2, lax.rem(k, 2)], me, lax.rem(k, 2), k // 2)
 
-        @pl.when(k == 2)
+        @pl.when(k == 1)
         def _():
             half_copy.wait_recv()
 
             def add_half(block, carry):
-                sums[block] = terms_ref[core, block] + sums_in[block]
+                sums[block] = terms_ref[core, block] + sums[block]
                 sums_low[block] = sums[block].astype(jnp.bfloat16)
                 return carry
 
@@ -248,24 +349,21 @@
             final[core] = summed
             final_copy(core).start()
 
-        @pl.when((k >= 1) & (k < last + 1))
-        def _():
-            now = k - 1
-            expert = lax.rem(now, 2)
-            pair_copy(now, third_pair).wait_recv()
-            core_copy(2, now, mine).start()
-            core_copy(0, now, others).wait_recv()
-            core_copy(1, now, others).wait_recv()
-            first, second = owner_right(now), owner_left(now)
+        @pl.when(k < last)
+        def _():
+            expert = lax.rem(k, 2)
+            core_copy(0, k, others).wait_recv()
+            core_copy(1, k, others).wait_recv()
+            first, second = owner_right(k), owner_left(k)
             for base in (mine, others):
                 part = base + third_right
                 add_product(weights[first, part, expert], first, expert, part)
                 part = base + third_left
                 add_product(weights[second, part, expert], second, expert, part)
 
-        @pl.when(k >= 2)
-        def _():
-            now = k - 2
+        @pl.when(k >= 1)
+        def _():
+            now = k - 1
             expert = lax.rem(now, 2)
             core_copy(2, now, others).wait_recv()
             owner = owner_right(now)
@@ -275,7 +373,7 @@
 
         return carry
 
-    lax.fori_loop(0, last + 2, step, 0)
+    lax.fori_loop(0, last + 1, step, 0)
 
     for part in range(6):
         width = total.shape[2]
@@ -307,49 +405,33 @@
     columns = width // peers
     wide = lane_padded(columns)
     split = counts[0, 0]
-    pad = ((0, 0), (0, 0), (0, wide - columns))
-    own = jnp.pad(dequantize(values, scales), pad)
-    own = own.reshape(EXPERTS_ACTIVE, 6, units // 6, wide).transpose(1, 0, 2, 3)
-    gated = (gates[:, None] * output_gradient.astype(jnp.float32)).astype(jnp.bfloat16)
-    blocks = jnp.pad(gated.reshape(rows, peers, columns), pad).transpose(1, 0, 2)
-    row_ids = lax.broadcasted_iota(jnp.int32, (rows, 1), 0)
-    first = row_ids < split
-    zero = jnp.zeros((), jnp.bfloat16)
-    masked = jnp.stack(
-        [
-            jnp.where(first[None, :CAP], blocks[:, :CAP], zero),
-            jnp.where(first[None, rows - CAP:], zero, blocks[:, rows - CAP:]),
-        ]
-    )
-    maps_in = jnp.concatenate([adapter_input_maps[0], adapter_input_maps[1]], axis=1)
-    maps_out = adapter_output_maps.reshape(EXPERTS_ACTIVE * rank, width)
-    of_expert = first == (lax.broadcasted_iota(jnp.int32, (1, EXPERTS_ACTIVE * rank), 1) < rank)
-    low_in = jnp.dot(hidden, maps_in, preferred_element_type=jnp.float32)
-    low_in = jnp.where(of_expert, low_in, 0.0).astype(jnp.bfloat16)
-    low_back = jnp.einsum("rd,kd->rk", gated, maps_out, preferred_element_type=jnp.float32)
-    low_back = jnp.where(of_expert, low_back, 0.0).astype(jnp.bfloat16)
-    term_a = jnp.einsum("rh,rk->hk", hidden, low_back, preferred_element_type=jnp.float32)
-    term_b = jnp.einsum("jrd,rk->jdk", blocks, low_in, preferred_element_type=jnp.float32)
-    terms = jnp.concatenate([term_a.reshape(peers, units // peers, -1), term_b], axis=1)
-    tall = terms.shape[1]
-    terms = terms.reshape(peers, 2, tall // 2, 2 * rank).transpose(1, 0, 2, 3)
-    maps_parts = maps_in.reshape(6, units // 6, 2 * rank)
+    first = lax.broadcasted_iota(jnp.int32, (1, rows, 1), 1) < split
+    of_expert = first == (lax.broadcasted_iota(jnp.int32, (EXPERTS_ACTIVE, 1, 1), 0) == 0)
+    expert_gates = jnp.where(of_expert, gates[None, :, None], 0.0)
+    parts = (EXPERTS_ACTIVE, 6, units // 6)
+    cut = units // peers
     last = 2 * (peers - 1)
-    half = (tall // 2, 2 * rank)
+    half = (rank, wide + lane_padded(cut))
     dma = pltpu.SemaphoreType.DMA
     vmem = pl.BlockSpec(memory_space=pltpu.VMEM)
     grad_hidden, summed = pl.pallas_call(
-        functools.partial(ring_kernel, peers),
+        functools.partial(ring_kernel, peers, columns),
         out_shape=(
             jax.ShapeDtypeStruct((rows, units), jnp.bfloat16),
             jax.ShapeDtypeStruct((2,) + half, jnp.float32),
         ),
-        in_specs=[vmem] * 5,
+        in_specs=[pl.BlockSpec(memory_space=pl.ANY)] * 2 + [vmem] * 5,
         out_specs=(vmem, vmem),
         scratch_shapes=[
-            pltpu.VMEM((peers,) + own.shape, jnp.bfloat16),
+            pltpu.VMEM((rows, width), jnp.bfloat16),
+            pltpu.VMEM((rows, units), jnp.bfloat16),
+            pltpu.VMEM((6, EXPERTS_ACTIVE, units // 6, wide), jnp.bfloat16),
+            pltpu.VMEM((EXPERTS_ACTIVE, peers, CAP, wide), jnp.bfloat16),
+            pltpu.VMEM((EXPERTS_ACTIVE, CAP, rank), jnp.bfloat16),
+            pltpu.VMEM((EXPERTS_ACTIVE, CAP, rank), jnp.bfloat16),
+            pltpu.VMEM((EXPERTS_ACTIVE, peers) + half, jnp.float32),
+            pltpu.VMEM((peers, 6, EXPERTS_ACTIVE, units // 6, wide), jnp.bfloat16),
             pltpu.VMEM((6, rows, units // 6), jnp.float32),
-            pltpu.VMEM((peers,) + half, jnp.float32),
             pltpu.VMEM((peers,) + half, jnp.float32),
             pltpu.VMEM((peers,) + half, jnp.bfloat16),
             pltpu.VMEM((peers - 1,) + half, jnp.bfloat16),
@@ -359,18 +441,25 @@
         + [dma((3, last))] * 2
         + [dma, dma]
         + [dma((peers - 1,))] * 2
-        + [dma, dma],
+        + [dma, dma, dma((2,))],
         compiler_params=pltpu.CompilerParams(
             collective_id=0, has_side_effects=True, vmem_limit_bytes=58 * 2**20
         ),
         cost_estimate=pl.CostEstimate(
             flops=2 * EXPERTS_ACTIVE * CAP * width * units, bytes_accessed=20 * 2**20, transcendentals=0
         ),
-    )(own, masked, low_back, maps_parts, terms)
-    summed = adapter_scale * summed.reshape(tall, EXPERTS_ACTIVE, rank)
-    cut = units // peers
-    grad_a = summed[:cut].transpose(1, 0, 2)
-    grad_b = summed[cut:cut + columns].transpose(1, 2, 0)
+    )(
+        output_gradient,
+        hidden,
+        expert_gates,
+        values.reshape(parts + (columns,)),
+        scales.reshape(EXPERTS_ACTIVE, 6, -1, columns),
+        adapter_input_maps.reshape(parts + (rank,)),
+        adapter_output_maps,
+    )
+    summed = adapter_scale * summed
+    grad_a = summed[:, :, wide:wide + cut].transpose(0, 2, 1)
+    grad_b = summed[:, :, :columns]
     return grad_hidden, grad_a, grad_b
 
 

time: 158 us -> 123 us (0.78)
  other arithmetic: 22.8 us -> 3.68 us
  matrix products: 13.1 us -> 0 us
  local copies, waits for them, and re-layouts: 27.5 us -> 19.4 us
  Pallas kernels: 93.5 us -> 98.6 us
    dot_general x3 -> x0, matrix products: 13.1 us -> none  [the longest x1 7.37 us: per_device_ring(): jnp.einsum('jrd,rk->jdk', blocks, low_in, preferred_element_type=jnp.floa...]
    reshape x3 -> x0, local copies, waits for them, and re-layouts: 11.6 us -> none  [the longest x1 8.27 us: per_device_ring(): gated.reshape(rows, peers, columns)]
    another operation x2 -> x0, other arithmetic: 11.5 us -> none  [per_device_ring(): jnp.stack([jnp.where(first[None, :CAP], blocks[:, :CAP], zero), jnp.where...]
    unnamed x18 -> x4, local copies, waits for them, and re-layouts: 6.62 us -> 18 us
    convert_element_type x1 -> x0, other arithmetic: 5.8 us -> none  [per_device_ring(): (gates[:, None] * output_gradient.astype(jnp.float32)).astype(jnp.bfloat16)]
    pallas_call x1, Pallas kernels: 93.5 us -> 98.6 us  [per_device_ring(): pl.pallas_call(functools.partial(ring_kernel, peers, columns), out_shape=...]
    transpose x3 -> x1, local copies, waits for them, and re-layouts: 4.66 us -> 0.66 us  [per_device_ring(): grad_a = summed[:, :, wide:wide + cut].transpose(0, 2, 1)]
    concatenate x2 -> x0, other arithmetic: 2.58 us -> none  [the longest x1 1.58 us: per_device_ring(): jnp.concatenate([term_a.reshape(peers, units // peers, -1), term_b], axis=1)]
where the time goes in v2:
time: 123 us; the launch traced here: 122 us
  Pallas kernels  98.6 us (80%)
  local copies, waits for them, and re-layouts  19.4 us (16%)
  other arithmetic  3.68 us (3%)
    pallas_call x1, Pallas kernels, per_device_ring(): pl.pallas_call(functools.partial(ring_kernel, peers, columns), out_shape=...  98.6 us
    unnamed x4, local copies, waits for them, and re-layouts  18 us

profile of v2, /device:TPU:16, one launch (start us, length us, event | category | flops | bytes accessed | tf_op | source)
XLA Modules:
  0.0 122.3 jit_solution(62792610134462225)
XLA Ops:
  0.6 0.7 iota_compare_fusion
  1.3 2.2 %copy.12 = bf16[2,1536,64]{2,1,0:T(8,128)(2,1)} copy(bf16[2,1536,64]{1,2,0:T(8,128)(2,1)} %param.14) | data formatting | bytes 786432 | tf_op args[6]
  3.5 2.0 %compare_select_fusion.gates_ref = f32[2,896,1]{2,1,0:T(8,128)} fusion(f32[896]{0:T(1024)} %param.10, pred[2]{0:T(512)(128)(4,1)S(1)} %iota_compare_fusion.1, pred[896]{0:T(1024)(128)(4,1)S(1)} %iota_compare_fusion), kind=kLoop, calls=%fused_computation | loop fusion | flops 3584 | bytes 11650 | tf_op jit(solution)/shard_map/jit(_where)/select_n | solution.py:410
  5.5 4.2 %copy.11 = bf16[2,1536,360]{2,1,0:T(8,128)(2,1)} copy(bf16[2,1536,360]{1,2,0:T(8,128)(2,1)} %param.12) | data formatting | bytes 4423680 | tf_op args[4]
  9.7 8.1 %copy.13.gradient_hbm = bf16[896,2880]{1,0:T(8,128)(2,1)} copy(bf16[896,2880]{0,1:T(8,128)(2,1)} %param.8) | data formatting | bytes 10321920 | tf_op args[0]
  17.9 98.6 %shard_map.103 = (bf16[896,1536]{1,0:T(8,128)(2,1)}, f32[2,64,640]{2,1,0:T(8,128)}) custom-call(bf16[896,2880]{1,0:T(8,128)(2,1)} %copy.13.gradient_hbm, bf16[896,1536]{1,0:T(8,128)(2,1)} %hidden_hbm.1, f32[2,896,1]{2,1,0:T(8,128)} %compare_select_fusion.gates_ref, bf16[2,6,256,360]{3,2,1,0:T(8,128)(2,1)} %bitcast.7, bf16[2,6,8,360]{3,2,1,0:T(8,128)(2,1)} %bitcast.9, ...), custom_call_target="tpu_custom_call" | custom-call | flops 11890851840 | bytes 20971520 | tf_op jit(solution)/shard_map/pallas_call | solution.py:417
  116.5 1.0 broadcast_multiply_fusion
  117.5 0.7 slice_bitcast_fusion
  118.2 0.7 slice.13
  118.9 3.5 %copy.15 = bf16[896,1536]{1,0:T(8,128)(2,1)} copy(bf16[896,1536]{1,0:T(8,128)(2,1)} %get-tuple-element.10) | data formatting | bytes 5505024
  (1 shorter events, 0.0 us)
